TPU v7x, 32 devices: a whole 2x2x4 slice. The times are simulated.
32 devices in a mesh: comp: 2 (over core), seq: 8 (over z, y), tp: 2 (over x).
Axes of the slice: x: 2, y: 2, z: 4, core: 2. Of those that a mesh axis runs over, the one named last changes fastest.
Arguments:
- inputs: bfloat16 [2, 8, 1024, 3072], P('comp', None, ('seq', 'tp')), may hold values from -6 to 6
- modulation: float32 [2, 8, 3, 3072], P('comp'), may hold values from -4 to 4
- w_qkv: bfloat16 [2, 3072, 3, 3072], P('comp', None, None, 'tp'), may hold values from -0.108253175 to 0.108253175
- w_attn_out: bfloat16 [2, 3072, 3072], P('comp', 'tp'), may hold values from -0.109375 to 0.109375
- qk_gain: float32 [2, 2, 128], P('comp'), may hold values from 1 to 5
- final_mod: float32 [8, 2, 3072], replicated, may hold values from -4 to 4
- w_final: bfloat16 [3072, 64], replicated, may hold values from -0.109375 to 0.109375
- w_embed: bfloat16 [64, 3072], replicated, may hold values from -0.75 to 0.75
- latent: float32 [8, 64, 1024], P(None, None, ('seq', 'tp')), may hold values from -6 to 6
Outputs:
- handed: bfloat16 [2, 8, 1024, 3072], P('comp', None, ('seq', 'tp'))
- velocity: float32 [8, 64, 1024], P(None, None, ('seq', 'tp'))
- advanced: float32 [8, 64, 1024], P(None, None, ('seq', 'tp'))
All inputs are finite; a program needn't handle non-finite values.
Results may differ from a plain program's by a relative error of at most 0.011.
Values may be sent and summed in bfloat16 or wider, within the bound.
A program may use at most 256 MiB of HBM per device.

v0:
```python
import jax
import jax.numpy as jnp
from jax import lax
from jax.sharding import PartitionSpec as P

step_size = 0.02
norm_eps = 1e-06


def broadcast(block, axis, owner):
    block = jnp.where(lax.axis_index(axis) == owner, block, jnp.zeros_like(block))
    return lax.psum(block, axis)


def shifted(block, axis, distance):
    devices = range(lax.axis_size(axis))
    route = [((i - distance) % len(devices), i) for i in devices]
    return lax.ppermute(block, axis, route)


def layer_norm(values):
    center = values - jnp.mean(values, -1, keepdims=True)
    return center * lax.rsqrt(jnp.mean(center * center, -1, keepdims=True) + norm_eps)


def rms_norm(values, norm_gain):
    return values * lax.rsqrt(jnp.mean(values * values, -1, keepdims=True) + norm_eps) * norm_gain


def body(inputs, modulation, w_qkv, w_attn_out, qk_gain, final_mod, w_final, w_embed, latent):
    head_dim = qk_gain.shape[2]
    x_rows = inputs[0]
    samples = x_rows.shape[0]
    mod_rows = modulation[0]
    x_float = x_rows.astype(jnp.float32)
    x_mod = (
        layer_norm(x_float) * (1.0 + mod_rows[:, 1, None, :]) + mod_rows[:, 0, None, :]
    ).astype(jnp.bfloat16)
    weights = w_qkv[0]
    local_width = weights.shape[2]
    heads_local = local_width // head_dim
    norm_gains = qk_gain[0]
    scaling = head_dim ** (-0.5)
    mixed_rows = jnp.einsum(
        "srd,dje->srje",
        lax.all_gather(x_mod, "tp", axis=1, tiled=True),
        weights,
        preferred_element_type=jnp.float32,
    )
    unpacked = mixed_rows.reshape(
        mixed_rows.shape[0], mixed_rows.shape[1], 3, heads_local, head_dim
    )
    project_queried = rms_norm(unpacked[:, :, 0], norm_gains[0])
    keyed_rows = rms_norm(unpacked[:, :, 1], norm_gains[1])
    projected = jnp.stack([project_queried, keyed_rows, unpacked[:, :, 2]], 2).astype(jnp.bfloat16)
    queried = projected[:, :, 0]
    query_count = queried.shape[1]
    pairs = projected[:, :, 1:]
    start_max = jnp.full((samples, query_count, heads_local), -1e30, jnp.float32)
    shard_piece = lax.all_gather(pairs, "seq", axis=1, tiled=True)
    run_max = start_max
    scores = (
        jnp.einsum(
            "sqhd,skhd->sqhk", queried, shard_piece[:, :, 0], preferred_element_type=jnp.float32
        )
        * scaling
    )
    new_max = jnp.maximum(run_max, jnp.max(scores, -1))
    weight = jnp.exp(scores - new_max[..., None])
    run_sum = jnp.sum(weight, -1)
    summed = jnp.einsum(
        "sqhk,skhd->sqhd",
        weight.astype(jnp.bfloat16),
        shard_piece[:, :, 1],
        preferred_element_type=jnp.float32,
    )
    run_acc = summed
    run_max, run_sum, run_acc = (new_max, run_sum, run_acc)
    attended = (
        (run_acc / run_sum[..., None])
        .astype(jnp.bfloat16)
        .reshape(samples, query_count, local_width)
    )
    partial_out = jnp.einsum(
        "sqe,ed->sqd", attended, w_attn_out[0], preferred_element_type=jnp.float32
    )
    branch = lax.psum_scatter(
        partial_out.astype(jnp.bfloat16), "tp", scatter_dimension=1, tiled=True
    ).astype(jnp.float32)
    output = (x_float + mod_rows[:, 2, None, :] * branch).astype(jnp.bfloat16)
    final_in = (
        layer_norm(output.astype(jnp.float32)) * (1.0 + final_mod[:, 1, None, :])
        + final_mod[:, 0, None, :]
    ).astype(jnp.bfloat16)
    velocity = jnp.einsum("srd,dc->scr", final_in, w_final, preferred_element_type=jnp.float32)
    advanced = latent + step_size * velocity
    last_comp = lax.axis_size("comp") - 1
    position = lax.axis_index("comp")
    shared = broadcast(
        jnp.stack([velocity, advanced]).astype(jnp.bfloat16), "comp", last_comp
    ).astype(jnp.float32)
    embedded = jnp.einsum(
        "scr,cd->srd", advanced.astype(jnp.bfloat16), w_embed, preferred_element_type=jnp.float32
    ).astype(jnp.bfloat16)
    sending = jnp.where(position == last_comp, embedded, output)
    handed = shifted(sending, "comp", 1)
    return (handed[None], shared[0], shared[1])


def solution(mesh):
    in_specs = (
        P("comp", None, ("seq", "tp"), None),
        P("comp", None, None, None),
        P("comp", None, None, "tp"),
        P("comp", "tp", None),
        P("comp", None, None),
        P(),
        P(),
        P(),
        P(None, None, ("seq", "tp")),
    )
    out_specs = (
        P("comp", None, ("seq", "tp"), None),
        P(None, None, ("seq", "tp")),
        P(None, None, ("seq", "tp")),
    )
    return jax.shard_map(body, mesh=mesh, in_specs=in_specs, out_specs=out_specs, check_vma=False)
```

profile of v0, /device:TPU:0, one launch (start us, length us, event | category | flops | bytes accessed | tf_op | source)
XLA Modules:
  0.0 1317.3 jit_solution(5315490603374308370)
XLA Ops:
  7.2 1.8 slice_bitcast_fusion.9
  9.0 2.4 convert_reduce_fusion.1
  11.4 2.8 fusion.20
  14.3 3.5 fusion.23
  18.1 37.0 %copy.21 = bf16[1,3072,3,1536]{1,3,2,0:T(8,128)(2,1)} copy(bf16[1,3072,3,1536]{3,1,2,0:T(8,128)(2,1)} %param.11) | data formatting | bytes 56623104 | tf_op args[2]
  55.1 45.9 %all-gather.3.cloned.1.call-done = bf16[8,128,3072]{2,1,0:T(8,128)(2,1)} async-done(((bf16[8,64,3072]{2,1,0:T(8,128)(2,1)}), bf16[8,128,3072]{2,1,0:T(8,128)(2,1)}) %all-gather.3.cloned.1.call-update) | async-done | bytes 6291472 | tf_op jit(solution)/shard_map/all_gather | solution.py:46
  101.1 35.4 %fusion.25 = f32[8,128,3,12,128]{1,4,3,2,0:T(8,128)S(1)} fusion(bf16[3,12,128,3072,1]{3,2,1,0,4:T(8,128)(2,1)} %bitcast.112, bf16[8,128,3072]{2,1,0:T(8,128)(2,1)} %all-gather.3.cloned.1.call-done), kind=kOutput, calls=%fused_computation.34 | convolution fusion | flops 28991029248 | bytes 53477376 | tf_op jit(solution)/shard_map/srd,dje->srje/dot_general | solution.py:44
  136.5 2.2 multiply_reduce_fusion
  138.6 3.0 slice.102
  141.6 2.2 copy-done.3
  143.9 3.0 multiply_convert_fusion.1
  146.8 6.0 pad_maximum_fusion
  153.2 953.5 %all-gather.5.cloned.1.call-done = bf16[8,1024,2,12,128]{1,4,3,2,0:T(8,128)(2,1)} async-done(((bf16[8,128,2,12,128]{1,4,3,2,0:T(8,128)(2,1)}), bf16[8,1024,2,12,128]{1,4,3,2,0:T(8,128)(2,1)}) %all-gather.5.cloned.1.call-update) | async-done | bytes 50331664 | tf_op jit(solution)/shard_map/all_gather | solution.py:60
  1106.7 28.2 %bitcast_reduce_fusion = (f32[8,128,12]{1,2,0:T(8,128)S(1)}, f32[8,12,1024,128]{3,2,1,0:T(8,128)}) fusion(f32[8,128,3,12,128]{1,4,3,2,0:T(8,128)} %copy-done.3, f32[128]{0:T(128)S(1)} %get-tuple-element.20, f32[8,128,12]{1,2,0:T(8,128)S(1)} %add_rsqrt_fusion, bf16[8,1024,2,12,128]{1,4,3,2,0:T(8,128)(2,1)} %all-gather.5.cloned.1.call-done), kind=kOutput, calls=%fused_computation.1 | convolution fusion | flops 3251097600 | bytes 81887744 | tf_op jit(solution)/shard_map/sqhd,skhd->sqhk/dot_general | solution.py:63
  1134.9 19.9 %fusion.1 = f32[8,128,12]{1,2,0:T(8,128)S(1)} fusion(f32[8,12,1024,128]{3,2,1,0:T(8,128)} %get-tuple-element.23, f32[8,128,12]{1,2,0:T(8,128)S(1)} %broadcast_maximum_fusion), kind=kLoop, calls=%fused_computation.3 | loop fusion | flops 37736448 | bytes 50429952 | tf_op jit(solution)/shard_map/reduce_sum | solution.py:70
  1154.8 27.9 %fusion.27 = bf16[8,128,12,128]{1,3,2,0:T(8,128)(2,1)} fusion(f32[8,128,12]{1,2,0:T(8,128)S(1)} %fusion.1, f32[8,12,1024,128]{3,2,1,0:T(8,128)} %get-tuple-element.23, f32[8,128,12]{1,2,0:T(8,128)S(1)} %broadcast_maximum_fusion, bf16[8,1024,2,12,128]{1,4,3,2,0:T(8,128)(2,1)} %all-gather.5.cloned.1.call-done), kind=kOutput, calls=%fused_computation.37 | convolution fusion | flops 3262119936 | bytes 78741504 | tf_op jit(solution)/shard_map/sqhk,skhd->sqhd/dot_general | solution.py:71
  1182.7 15.3 %fusion.28 = bf16[8,128,3072]{2,1,0:T(8,128)(2,1)} fusion(bf16[8,128,1536]{1,2,0:T(8,128)(2,1)} %bitcast.116, bf16[1,1536,3072]{2,1,0:T(8,128)(2,1)} %param.12), kind=kOutput, calls=%fused_computation.42 | convolution fusion | flops 9666822144 | bytes 18874368 | tf_op jit(solution)/shard_map/sqe,ed->sqd/dot_general | solution.py:84
  1198.4 2.0 copy.28
  1202.3 73.1 %reduce-scatter.2.cloned.1.call-done = bf16[8,64,3072]{2,1,0:T(8,128)(2,1)} async-done(((bf16[8,128,3072]{2,1,0:T(8,128)(2,1)}), bf16[8,64,3072]{2,1,0:T(8,128)(2,1)}) %reduce-scatter.2.cloned.1.call-update) | async-done | bytes 3145744 | tf_op jit(solution)/shard_map/reduce_scatter | solution.py:87
  1275.3 3.5 convert_reduce_fusion
  1283.1 18.6 %all-reduce.2.cloned.1.call-done = bf16[2,8,64,64]{2,3,1,0:T(8,128)(2,1)} async-done(((bf16[2,8,64,64]{2,3,1,0:T(8,128)(2,1)}), bf16[2,8,64,64]{2,3,1,0:T(8,128)(2,1)}) %all-reduce.2.cloned.1.call-update) | async-done | bytes 131088 | tf_op jit(solution)/shard_map/psum | solution.py:12
  1303.5 1.8 copy.29
  1305.2 1.8 copy.30
  1307.0 3.8 copy.44
  (43 shorter events, 8.9 us)
Async XLA Ops:
  7.2 1274.1 %copy-start = (bf16[64,3072]{1,0:T(8,128)(2,1)S(1)}, bf16[64,3072]{1,0:T(8,128)(2,1)}, u32[]{:S(2)}) copy-start(bf16[64,3072]{1,0:T(8,128)(2,1)} %param.16) | copy-start | bytes 1179652
  7.2 7.1 copy-start.1
  7.2 93.9 %all-gather.3.cloned.1.call-start = ((), (), s32[]{:S(2)}) async-start(), calls=%async_computation.1 | async-start | bytes 9437184 | tf_op jit(solution)/shard_map/all_gather | solution.py:46
  17.9 37.3 %copy-start.7 = (f32[1,2,128]{2,1,0:T(2,128)S(1)}, f32[1,2,128]{2,1,0:T(2,128)}, u32[]{:S(2)}) copy-start(f32[1,2,128]{2,1,0:T(2,128)} %param.13) | copy-start | bytes 3076
  17.9 1088.8 %all-gather.5.cloned.1.call-start = ((), (), s32[]{:S(2)}) async-start(), calls=%async_computation.2 | async-start | bytes 56623104 | tf_op jit(solution)/shard_map/all_gather | solution.py:60
  136.5 7.4 copy-start.3
  152.9 1122.4 %reduce-scatter.2.cloned.1.call-start = ((), (), s32[]{:S(2)}) async-start(), calls=%async_computation.3 | async-start | bytes 9437184 | tf_op jit(solution)/shard_map/reduce_scatter | solution.py:87
  1198.1 77.3 %copy-start.2 = (bf16[1,8,64,3072]{3,2,1,0:T(8,128)(2,1)S(1)}, bf16[1,8,64,3072]{3,2,1,0:T(8,128)(2,1)}, u32[]{:S(2)}) copy-start(bf16[1,8,64,3072]{3,2,1,0:T(8,128)(2,1)} %param.9) | copy-start | bytes 9437188
  1198.1 103.6 %all-reduce.2.cloned.1.call-start = ((), (), s32[]{:S(2)}) async-start(), calls=%async_computation.4 | async-start | bytes 524288 | tf_op jit(solution)/shard_map/psum | solution.py:12
  1275.3 4.5 copy-start.4
  1275.3 4.5 copy-start.5
  1275.3 4.5 copy-start.6
  1275.3 4.5 copy-start.8
  1282.2 24.8 %collective-permute-start = (bf16[8,64,3072]{2,1,0:T(8,128)(2,1)S(1)}, bf16[8,64,3072]{2,1,0:T(8,128)(2,1)}, u32[]{:S(2)}, u32[]{:S(2)}) collective-permute-start(bf16[8,64,3072]{2,1,0:T(8,128)(2,1)S(1)} %fusion.31), channel_id=1, source_target_pairs={{16,0},{0,16},{17,1},{1,17},{18,2},{2,18},{19,3},{3,19},{20,4},{4,... | collective-permute-start | bytes 9437192 | tf_op jit(solution)/shard_map/ppermute | solution.py:18
Sparse Core Ops, SparseCore 0:
  18.0 83.0 all-gather.2
  153.0 953.6 all-gather.4
  1198.2 77.0 reduce-scatter.1
  1283.2 18.4 all-reduce.1
where the time goes:
time: 1320 us
  waiting for transfers between devices  1090 us (83%)
  matrix products  109 us (8%)
  local copies, waits for them, and re-layouts  53.6 us (4%)
  other arithmetic  48.5 us (4%)
  between operations  13.9 us (1%)
    all_gather x1, waiting for transfers between devices, body(): shard_piece = lax.all_gather(pairs, 'seq', axis=1, tiled=True)  954 us
    reduce_scatter x1, waiting for transfers between devices, body(): lax.psum_scatter(partial_out.astype(jnp.bfloat16), 'tp', scatter_dimensio...  73.1 us
    unnamed x23, local copies, waits for them, and re-layouts  48.6 us
    all_gather x1, waiting for transfers between devices, body(): lax.all_gather(x_mod, 'tp', axis=1, tiled=True)  45.9 us
    dot_general x1, matrix products, body(): jnp.einsum('srd,dje->srje', lax.all_gather(x_mod, 'tp', axis=1, tiled=Tru...  35.4 us
    dot_general x1, matrix products, body(): jnp.einsum('sqhd,skhd->sqhk', queried, shard_piece[:, :, 0], preferred_el...  28.2 us
    dot_general x1, matrix products, body(): jnp.einsum('sqhk,skhd->sqhd', weight.astype(jnp.bfloat16), shard_piece[:,...  27.9 us
  transfers between devices with their start and end apart: 5, of which 4 were waited for; matrix products, arithmetic and copies ran while one was open for 4% of the time, Pallas kernels for 0%

commit v1 on v0

--- a/solution.py
+++ b/solution.py
@@ -107,6 +107,97 @@
     return (handed[None], shared[0], shared[1])
 
 
+def by_clip(inputs, modulation, w_qkv, w_attn_out, qk_gain, final_mod, w_final, w_embed, latent):
+    head_dim = qk_gain.shape[2]
+    x_rows = inputs[0]
+    samples, block, width = x_rows.shape
+    clip = lax.axis_index("seq")
+    comp = lax.axis_index("comp")
+    comps = lax.axis_size("comp")
+    tps = lax.axis_size("tp")
+    sent = [
+        lax.dynamic_index_in_dim(x_rows, lax.rem(clip + d, samples), 0, False)
+        for d in range(samples)
+    ]
+    got = []
+    for d in range(samples):
+        route = [(i, (i + d) % samples) for i in range(samples)]
+        got.append(lax.ppermute(sent[d], "seq", route) if d else sent[0])
+    own_raw = jnp.concatenate(got, 0)
+    mod = lax.dynamic_index_in_dim(modulation[0], clip, 0, False)
+    own_float = own_raw.astype(jnp.float32)
+    x_mod = (layer_norm(own_float) * (1.0 + mod[1]) + mod[0]).astype(jnp.bfloat16)
+    x_full = lax.all_gather(x_mod, "tp", axis=0, tiled=True)
+    rows = x_full.shape[0]
+    weights = w_qkv[0]
+    local_width = weights.shape[2]
+    heads_local = local_width // head_dim
+    mixed = jnp.einsum("rd,dje->jre", x_full, weights, preferred_element_type=jnp.float32)
+    unpacked = mixed.reshape(3, rows, heads_local, head_dim)
+    queried = rms_norm(unpacked[0], qk_gain[0, 0]).astype(jnp.bfloat16)
+    keyed = rms_norm(unpacked[1], qk_gain[0, 1]).astype(jnp.bfloat16)
+    valued = unpacked[2].astype(jnp.bfloat16)
+    scores = jnp.einsum("qhd,khd->hqk", queried, keyed, preferred_element_type=jnp.float32) * (
+        head_dim ** (-0.5)
+    )
+    weight = jnp.exp(scores - jnp.max(scores, -1, keepdims=True))
+    total = jnp.sum(weight, -1)
+    summed = jnp.einsum(
+        "hqk,khd->qhd", weight.astype(jnp.bfloat16), valued, preferred_element_type=jnp.float32
+    )
+    attended = (summed / total.T[..., None]).astype(jnp.bfloat16).reshape(rows, local_width)
+    partial_out = jnp.dot(attended, w_attn_out[0], preferred_element_type=jnp.float32)
+    branch = lax.psum_scatter(
+        partial_out.astype(jnp.bfloat16), "tp", scatter_dimension=0, tiled=True
+    ).astype(jnp.float32)
+    output = (own_float + mod[2] * branch).astype(jnp.bfloat16)
+    return finish(output, samples, block, width, clip, comp, comps, final_mod, w_final, w_embed, latent)
+
+
+def rolled(blocks, clip, samples):
+    twice = jnp.concatenate([blocks, blocks], 0)
+    return lax.dynamic_slice_in_dim(twice, lax.rem(samples - clip, samples), samples, 0)
+
+
+def finish(output, samples, block, width, clip, comp, comps, final_mod, w_final, w_embed, latent):
+    last = comps - 1
+    fmod = lax.dynamic_index_in_dim(final_mod, clip, 0, False)
+    final_in = (layer_norm(output.astype(jnp.float32)) * (1.0 + fmod[1]) + fmod[0]).astype(
+        jnp.bfloat16
+    )
+    speed = jnp.dot(final_in, w_final, preferred_element_type=jnp.float32)
+    channels = speed.shape[-1]
+    slots = output.reshape(samples, block, width)
+    speeds = speed.reshape(samples, block, channels)
+    home, moved = [], []
+    for d in range(samples):
+        route = [
+            (c * samples + i, (c + 1) * samples + (i - d) % samples)
+            for c in range(comps - 1)
+            for i in range(samples)
+        ]
+        home.append(lax.ppermute(slots[d], ("comp", "seq"), route))
+        part = speeds[d]
+        if d:
+            part = lax.ppermute(part, "seq", [(i, (i - d) % samples) for i in range(samples)])
+        moved.append(part)
+    velocity = rolled(jnp.stack(moved), clip, samples)
+    velocity = broadcast(velocity, "comp", last).transpose(0, 2, 1)
+    advanced = latent + step_size * velocity
+    embedded = jnp.einsum(
+        "scr,cd->srd", advanced.astype(jnp.bfloat16), w_embed, preferred_element_type=jnp.float32
+    ).astype(jnp.bfloat16)
+    returned = rolled(jnp.stack(home), clip, samples)
+    handed = jnp.where(comp == 0, embedded, returned)
+    return (handed[None], velocity, advanced)
+
+
+def plan(inputs, *rest):
+    if inputs.shape[1] == lax.axis_size("seq"):
+        return by_clip(inputs, *rest)
+    return body(inputs, *rest)
+
+
 def solution(mesh):
     in_specs = (
         P("comp", None, ("seq", "tp"), None),
@@ -124,4 +215,4 @@
         P(None, None, ("seq", "tp")),
         P(None, None, ("seq", "tp")),
     )
-    return jax.shard_map(body, mesh=mesh, in_specs=in_specs, out_specs=out_specs, check_vma=False)
+    return jax.shard_map(plan, mesh=mesh, in_specs=in_specs, out_specs=out_specs, check_vma=False)

time: 1320 us -> 502 us (0.38)
  waiting for transfers between devices: 1090 us -> 246 us
  starting transfers between devices: 0.9 us -> 52.3 us
  matrix products: 109 us -> 92.9 us
    all_gather x2 -> x1, waiting for transfers between devices: 999 us -> 84.1 us  [by_clip(): x_full = lax.all_gather(x_mod, 'tp', axis=0, tiled=True)]
    ppermute x1 -> x22, waiting for transfers between devices: 0.01 us -> 71.1 us  [the longest x7 48.8 us: by_clip(): got.append(lax.ppermute(sent[d], 'seq', route) if d else sent[0])]
    ppermute x1 -> x22, starting transfers between devices: 0.07 us -> 52 us  [the longest x8 20.3 us: finish(): home.append(lax.ppermute(slots[d], ('comp', 'seq'), route))]
    unnamed x23 -> x60, local copies, waits for them, and re-layouts: 48.6 us -> 13.6 us
    slice x2 -> x7, local copies, waits for them, and re-layouts: 4.17 us -> 31.7 us  [the longest x2 16.9 us: by_clip(): keyed = rms_norm(unpacked[1], qk_gain[0, 1]).astype(jnp.bfloat16)]
    dot_general x6, matrix products: 109 us -> 92.9 us  [the longest x1 34.5 us: by_clip(): jnp.einsum('rd,dje->jre', x_full, weights, preferred_element_type=jnp.flo...]
  transfers between devices with their start and end apart: 5 -> 25, of which waited for: 4 -> 11; matrix products, arithmetic and copies ran while one was open for 4% -> 2% of each run, Pallas kernels for 0% -> 0%
where the time goes in v1:
time: 502 us; the launch traced here: 498 us
  waiting for transfers between devices  246 us (49%)
  matrix products  92.9 us (19%)
  starting transfers between devices  52.3 us (10%)
  local copies, waits for them, and re-layouts  50.9 us (10%)
  other arithmetic  41.5 us (8%)
  between operations  14.4 us (3%)
    all_gather x1, waiting for transfers between devices, by_clip(): x_full = lax.all_gather(x_mod, 'tp', axis=0, tiled=True)  84.1 us
    reduce_scatter x1, waiting for transfers between devices, by_clip(): lax.psum_scatter(partial_out.astype(jnp.bfloat16), 'tp', scatter_dimensio...  75.7 us
    ppermute x7, waiting for transfers between devices, by_clip(): got.append(lax.ppermute(sent[d], 'seq', route) if d else sent[0])  48.8 us
    dot_general x1, matrix products, by_clip(): jnp.einsum('rd,dje->jre', x_full, weights, preferred_element_type=jnp.flo...  34.5 us
    dot_general x1, matrix products, by_clip(): jnp.einsum('qhd,khd->hqk', queried, keyed, preferred_element_type=jnp.flo...  20.9 us
    ppermute x8, starting transfers between devices, finish(): home.append(lax.ppermute(slots[d], ('comp', 'seq'), route))  20.3 us
    reduce_sum x1, other arithmetic, by_clip(): total = jnp.sum(weight, -1)  20 us
    dot_general x1, matrix products, by_clip(): jnp.einsum('hqk,khd->qhd', weight.astype(jnp.bfloat16), valued, preferred...  19 us
  transfers between devices with their start and end apart: 25, of which 11 were waited for; matrix products, arithmetic and copies ran while one was open for 2% of the time, Pallas kernels for 0%

profile of v1, /device:TPU:0, one launch (start us, length us, event | category | flops | bytes accessed | tf_op | source)
XLA Modules:
  0.0 497.9 jit_solution(16442633033021115188)
XLA Ops:
  10.6 6.0 %collective-permute-start.6 = (bf16[64,3072]{1,0:T(8,128)(2,1)}, bf16[64,3072]{1,0:T(8,128)(2,1)}, u32[]{:S(2)}, u32[]{:S(2)}) collective-permute-start(bf16[64,3072]{1,0:T(8,128)(2,1)} %get-tuple-element.15), channel_id=1, source_target_pairs={{0,14},{2,0},{4,2},{6,4},{8,6},{10,8},{12,10},{14,12},{1,15},{3,1}... | collective-permute-start | bytes 1179656 | tf_op jit(solution)/shard_map/ppermute | solution.py:125
  22.1 30.5 %collective-permute-done = bf16[64,3072]{1,0:T(8,128)(2,1)} collective-permute-done((bf16[64,3072]{1,0:T(8,128)(2,1)}, bf16[64,3072]{1,0:T(8,128)(2,1)}, u32[]{:S(2)}, u32[]{:S(2)}) %collective-permute-start) | collective-permute-done | bytes 393248 | tf_op jit(solution)/shard_map/ppermute | solution.py:125
  52.7 8.9 %collective-permute-start.2 = (bf16[64,3072]{1,0:T(8,128)(2,1)}, bf16[64,3072]{1,0:T(8,128)(2,1)S(1)}, u32[]{:S(2)}, u32[]{:S(2)}) collective-permute-start(bf16[64,3072]{1,0:T(8,128)(2,1)} %get-tuple-element.18), channel_id=1, source_target_pairs={{0,6},{2,8},{4,10},{6,12},{8,14},{10,0},{12,2},{14,4},{1,7},{3,9},... | collective-permute-start | bytes 1179656 | tf_op jit(solution)/shard_map/ppermute | solution.py:125
  63.7 14.5 %collective-permute-done.2 = bf16[64,3072]{1,0:T(8,128)(2,1)S(1)} collective-permute-done((bf16[64,3072]{1,0:T(8,128)(2,1)}, bf16[64,3072]{1,0:T(8,128)(2,1)S(1)}, u32[]{:S(2)}, u32[]{:S(2)}) %collective-permute-start.2) | collective-permute-done | bytes 393248 | tf_op jit(solution)/shard_map/ppermute | solution.py:125
  91.5 84.1 %all-gather.2.cloned.1.call-done = bf16[1024,3072]{1,0:T(8,128)(2,1)} async-done(((bf16[512,3072]{1,0:T(8,128)(2,1)}), bf16[1024,3072]{1,0:T(8,128)(2,1)}) %all-gather.2.cloned.1.call-update) | async-done | bytes 6291472 | tf_op jit(solution)/shard_map/all_gather | solution.py:130
  175.6 34.5 %fusion.10 = f32[3,1024,1536]{2,1,0:T(8,128)S(1)} fusion(bf16[1,3072,3,1536]{3,1,2,0:T(8,128)(2,1)} %param.11, bf16[1024,3072]{1,0:T(8,128)(2,1)} %all-gather.2.cloned.1.call-done), kind=kOutput, calls=%fused_computation.14 | convolution fusion | flops 28991029248 | bytes 53477376 | tf_op jit(solution)/shard_map/rd,dje->jre/dot_general | solution.py:135
  210.1 6.5 %copy-done.2 = f32[3,1024,1536]{2,1,0:T(8,128)} copy-done((f32[3,1024,1536]{2,1,0:T(8,128)}, f32[3,1024,1536]{2,1,0:T(8,128)S(1)}, u32[]{:S(2)}) %copy-start.2) | copy-done | bytes 18874392
  218.6 10.4 %fusion.46 = (f32[1,1024,1536]{2,1,0:T(8,128)}, f32[1,1024,1536]{2,1,0:T(8,128)}) fusion(f32[3,1024,1536]{2,1,0:T(8,128)} %copy-done.2), kind=kLoop, calls=%fused_computation.113 | loop fusion | bytes 25165824 | tf_op jit(solution)/shard_map/slice | solution.py:138
  229.0 6.6 %copy.19 = f32[1,1024,1536]{1,2,0:T(8,128)} copy(f32[1,1024,1536]{2,1,0:T(8,128)} %get-tuple-element.5) | data formatting | bytes 12582912 | tf_op jit(solution)/shard_map/slice | solution.py:138
  235.6 4.7 copy.17
  240.2 4.3 multiply_reduce_fusion.1
  244.5 6.6 %copy.18 = f32[1,1024,1536]{1,2,0:T(8,128)} copy(f32[1,1024,1536]{2,1,0:T(8,128)} %get-tuple-element.6) | data formatting | bytes 12582912 | tf_op jit(solution)/shard_map/slice | solution.py:137
  255.8 20.9 %multiply_reduce_fusion = (f32[12,1024]{1,0:T(8,128)S(1)}, f32[12,1024,1024]{1,2,0:T(8,128)}) fusion(f32[1024,12,128]{0,2,1:T(8,128)} %bitcast.113, f32[128]{0:T(128)S(1)} %copy-done.9, f32[1024,12]{0,1:T(8,128)S(1)} %get-tuple-element.38, f32[1024,12,128]{0,2,1:T(8,128)S(1)} %bitcast.115, f32[128]{0:T(128)S(1)} %get-tuple-element.34, ...), kind=kOutput, calls=%fused_computation.1 | convolution fusion | flops 3255816192 | bytes 63063040 | tf_op jit(solution)/shard_map/qhd,khd->hqk/dot_general | solution.py:140
  276.7 20.0 %fusion = f32[12,1024]{1,0:T(8,128)S(1)} fusion(f32[12,1024,1024]{1,2,0:T(8,128)} %get-tuple-element.37, f32[12,1024]{1,0:T(8,128)S(1)} %get-tuple-element.36), kind=kLoop, calls=%fused_computation.2 | loop fusion | flops 37736448 | bytes 50429952 | tf_op jit(solution)/shard_map/reduce_sum | solution.py:144
  296.7 19.0 %fusion.26 = bf16[1024,12,128]{0,2,1:T(8,128)(2,1)S(1)} fusion(f32[1024,12]{0,1:T(8,128)S(1)} %bitcast.117, bf16[1024,12,128]{0,2,1:T(8,128)(2,1)S(1)} %bitcast.116, f32[12,1024,1024]{1,2,0:T(8,128)} %get-tuple-element.37, f32[12,1024]{1,0:T(8,128)S(1)} %get-tuple-element.36), kind=kOutput, calls=%fused_computation.32 | convolution fusion | flops 3262119936 | bytes 56721408 | tf_op jit(solution)/shard_map/hqk,khd->qhd/dot_general | solution.py:145
  315.7 14.4 %fusion.28 = bf16[1024,3072]{1,0:T(8,128)(2,1)} fusion(bf16[1024,1536]{0,1:T(8,128)(2,1)S(1)} %bitcast.123, bf16[1,1536,3072]{2,1,0:T(8,128)(2,1)} %param.12), kind=kOutput, calls=%fused_computation.38 | convolution fusion | flops 9666822144 | bytes 18874368 | tf_op jit(solution)/shard_map/dot_general | solution.py:149
  331.6 75.7 %reduce-scatter.2.cloned.1.call-done = bf16[512,3072]{1,0:T(8,128)(2,1)} async-done(((bf16[1024,3072]{1,0:T(8,128)(2,1)}), bf16[512,3072]{1,0:T(8,128)(2,1)}) %reduce-scatter.2.cloned.1.call-update) | async-done | bytes 3145744 | tf_op jit(solution)/shard_map/reduce_scatter | solution.py:150
  414.6 4.3 collective-permute-start.7
  441.1 14.8 %all-reduce.2.cloned.1.call-done = f32[8,64,64]{2,1,0:T(8,128)} async-done(((f32[8,64,64]{2,1,0:T(8,128)}), f32[8,64,64]{2,1,0:T(8,128)}) %all-reduce.2.cloned.1.call-update) | async-done | bytes 131088 | tf_op jit(solution)/shard_map/psum | solution.py:12
  456.9 6.3 %collective-permute-start.15 = (bf16[64,3072]{1,0:T(8,128)(2,1)}, bf16[64,3072]{1,0:T(8,128)(2,1)S(1)}, u32[]{:S(2)}, u32[]{:S(2)}) collective-permute-start(bf16[64,3072]{1,0:T(8,128)(2,1)} %get-tuple-element.13), channel_id=1, source_target_pairs={{0,30},{2,16},{4,18},{6,20},{8,22},{10,24},{12,26},{14,28},{1,31},... | collective-permute-start | bytes 1179656 | tf_op jit(solution)/shard_map/ppermute | solution.py:179
  463.3 5.5 %collective-permute-done.15 = bf16[64,3072]{1,0:T(8,128)(2,1)S(1)} collective-permute-done((bf16[64,3072]{1,0:T(8,128)(2,1)}, bf16[64,3072]{1,0:T(8,128)(2,1)S(1)}, u32[]{:S(2)}, u32[]{:S(2)}) %collective-permute-start.15) | collective-permute-done | bytes 393248 | tf_op jit(solution)/shard_map/ppermute | solution.py:179
  471.7 5.5 %collective-permute-done.16 = bf16[64,3072]{1,0:T(8,128)(2,1)S(1)} collective-permute-done((bf16[64,3072]{1,0:T(8,128)(2,1)}, bf16[64,3072]{1,0:T(8,128)(2,1)S(1)}, u32[]{:S(2)}, u32[]{:S(2)}) %collective-permute-start.16) | collective-permute-done | bytes 393248 | tf_op jit(solution)/shard_map/ppermute | solution.py:179
  477.2 4.6 collective-permute-start.17
  481.9 5.5 %collective-permute-done.17 = bf16[64,3072]{1,0:T(8,128)(2,1)S(1)} collective-permute-done((bf16[64,3072]{1,0:T(8,128)(2,1)}, bf16[64,3072]{1,0:T(8,128)(2,1)S(1)}, u32[]{:S(2)}, u32[]{:S(2)}) %collective-permute-start.17) | collective-permute-done | bytes 393248 | tf_op jit(solution)/shard_map/ppermute | solution.py:179
  (124 shorter events, 69.4 us)
Async XLA Ops:
  7.2 168.4 %all-gather.2.cloned.1.call-start = ((), (), s32[]{:S(2)}) async-start(), calls=%async_computation.1 | async-start | bytes 9437184 | tf_op jit(solution)/shard_map/all_gather | solution.py:130
  10.6 73.5 %collective-permute-start.6 = (bf16[64,3072]{1,0:T(8,128)(2,1)}, bf16[64,3072]{1,0:T(8,128)(2,1)}, u32[]{:S(2)}, u32[]{:S(2)}) collective-permute-start(bf16[64,3072]{1,0:T(8,128)(2,1)} %get-tuple-element.15), channel_id=1, source_target_pairs={{0,14},{2,0},{4,2},{6,4},{8,6},{10,8},{12,10},{14,12},{1,15},{3,1}... | collective-permute-start | bytes 1179656 | tf_op jit(solution)/shard_map/ppermute | solution.py:125
  16.6 62.7 %collective-permute-start.4 = (bf16[64,3072]{1,0:T(8,128)(2,1)}, bf16[64,3072]{1,0:T(8,128)(2,1)}, u32[]{:S(2)}, u32[]{:S(2)}) collective-permute-start(bf16[64,3072]{1,0:T(8,128)(2,1)} %get-tuple-element.16), channel_id=1, source_target_pairs={{0,10},{2,12},{4,14},{6,0},{8,2},{10,4},{12,6},{14,8},{1,11},{3,13... | collective-permute-start | bytes 1179656 | tf_op jit(solution)/shard_map/ppermute | solution.py:125
  16.6 61.6 %collective-permute-start.3 = (bf16[64,3072]{1,0:T(8,128)(2,1)}, bf16[64,3072]{1,0:T(8,128)(2,1)}, u32[]{:S(2)}, u32[]{:S(2)}) collective-permute-start(bf16[64,3072]{1,0:T(8,128)(2,1)} %get-tuple-element.17), channel_id=1, source_target_pairs={{0,8},{2,10},{4,12},{6,14},{8,0},{10,2},{12,4},{14,6},{1,9},{3,11}... | collective-permute-start | bytes 1179656 | tf_op jit(solution)/shard_map/ppermute | solution.py:125
  16.6 46.0 %collective-permute-start.1 = (bf16[64,3072]{1,0:T(8,128)(2,1)}, bf16[64,3072]{1,0:T(8,128)(2,1)}, u32[]{:S(2)}, u32[]{:S(2)}) collective-permute-start(bf16[64,3072]{1,0:T(8,128)(2,1)} %get-tuple-element.19), channel_id=1, source_target_pairs={{0,4},{2,6},{4,8},{6,10},{8,12},{10,14},{12,0},{14,2},{1,5},{3,7},... | collective-permute-start | bytes 1179656 | tf_op jit(solution)/shard_map/ppermute | solution.py:125
  18.0 34.7 %collective-permute-start = (bf16[64,3072]{1,0:T(8,128)(2,1)}, bf16[64,3072]{1,0:T(8,128)(2,1)}, u32[]{:S(2)}, u32[]{:S(2)}) collective-permute-start(bf16[64,3072]{1,0:T(8,128)(2,1)} %get-tuple-element.20), channel_id=1, source_target_pairs={{0,2},{2,4},{4,6},{6,8},{8,10},{10,12},{12,14},{14,0},{1,3},{3,5},... | collective-permute-start | bytes 1179656 | tf_op jit(solution)/shard_map/ppermute | solution.py:125
  52.7 25.5 %collective-permute-start.2 = (bf16[64,3072]{1,0:T(8,128)(2,1)}, bf16[64,3072]{1,0:T(8,128)(2,1)S(1)}, u32[]{:S(2)}, u32[]{:S(2)}) collective-permute-start(bf16[64,3072]{1,0:T(8,128)(2,1)} %get-tuple-element.18), channel_id=1, source_target_pairs={{0,6},{2,8},{4,10},{6,12},{8,14},{10,0},{12,2},{14,4},{1,7},{3,9},... | collective-permute-start | bytes 1179656 | tf_op jit(solution)/shard_map/ppermute | solution.py:125
  62.6 21.5 %collective-permute-start.5 = (bf16[64,3072]{1,0:T(8,128)(2,1)}, bf16[64,3072]{1,0:T(8,128)(2,1)S(1)}, u32[]{:S(2)}, u32[]{:S(2)}) collective-permute-start(bf16[64,3072]{1,0:T(8,128)(2,1)} %get-tuple-element.21), channel_id=1, source_target_pairs={{0,12},{2,14},{4,0},{6,2},{8,4},{10,6},{12,8},{14,10},{1,13},{3,15... | collective-permute-start | bytes 1179656 | tf_op jit(solution)/shard_map/ppermute | solution.py:125
  90.0 317.2 %reduce-scatter.2.cloned.1.call-start = ((), (), s32[]{:S(2)}) async-start(), calls=%async_computation.2 | async-start | bytes 9437184 | tf_op jit(solution)/shard_map/reduce_scatter | solution.py:150
  330.1 125.8 %all-reduce.2.cloned.1.call-start = ((), (), s32[]{:S(2)}) async-start(), calls=%async_computation.3 | async-start | bytes 524288 | tf_op jit(solution)/shard_map/psum | solution.py:12
  414.6 9.6 %collective-permute-start.7 = (f32[64,64]{0,1:T(8,128)S(1)}, f32[64,64]{0,1:T(8,128)S(1)}, u32[]{:S(2)}, u32[]{:S(2)}) collective-permute-start(f32[64,64]{0,1:T(8,128)S(1)} %get-tuple-element.33), channel_id=1, source_target_pairs={{0,14},{2,0},{4,2},{6,4},{8,6},{10,8},{12,10},{14,12},{1,15},{3,1}... | collective-permute-start | bytes 49160 | tf_op jit(solution)/shard_map/ppermute | solution.py:182
  418.9 16.0 %collective-permute-start.13 = (f32[64,64]{0,1:T(8,128)S(1)}, f32[64,64]{0,1:T(8,128)S(1)}, u32[]{:S(2)}, u32[]{:S(2)}) collective-permute-start(f32[64,64]{0,1:T(8,128)S(1)} %get-tuple-element.27), channel_id=1, source_target_pairs={{0,2},{2,4},{4,6},{6,8},{8,10},{10,12},{12,14},{14,0},{1,3},{3,5},... | collective-permute-start | bytes 49160 | tf_op jit(solution)/shard_map/ppermute | solution.py:182
  418.9 16.0 %collective-permute-start.12 = (f32[64,64]{0,1:T(8,128)S(1)}, f32[64,64]{0,1:T(8,128)S(1)}, u32[]{:S(2)}, u32[]{:S(2)}) collective-permute-start(f32[64,64]{0,1:T(8,128)S(1)} %get-tuple-element.28), channel_id=1, source_target_pairs={{0,4},{2,6},{4,8},{6,10},{8,12},{10,14},{12,0},{14,2},{1,5},{3,7},... | collective-permute-start | bytes 49160 | tf_op jit(solution)/shard_map/ppermute | solution.py:182
  418.9 15.9 %collective-permute-start.11 = (f32[64,64]{0,1:T(8,128)S(1)}, f32[64,64]{0,1:T(8,128)S(1)}, u32[]{:S(2)}, u32[]{:S(2)}) collective-permute-start(f32[64,64]{0,1:T(8,128)S(1)} %get-tuple-element.29), channel_id=1, source_target_pairs={{0,6},{2,8},{4,10},{6,12},{8,14},{10,0},{12,2},{14,4},{1,7},{3,9},... | collective-permute-start | bytes 49160 | tf_op jit(solution)/shard_map/ppermute | solution.py:182
  421.4 13.4 %collective-permute-start.10 = (f32[64,64]{0,1:T(8,128)S(1)}, f32[64,64]{0,1:T(8,128)S(1)}, u32[]{:S(2)}, u32[]{:S(2)}) collective-permute-start(f32[64,64]{0,1:T(8,128)S(1)} %get-tuple-element.30), channel_id=1, source_target_pairs={{0,8},{2,10},{4,12},{6,14},{8,0},{10,2},{12,4},{14,6},{1,9},{3,11}... | collective-permute-start | bytes 49160 | tf_op jit(solution)/shard_map/ppermute | solution.py:182
  428.7 4.8 collective-permute-start.9
  433.5 23.4 %collective-permute-start.14 = (bf16[64,3072]{1,0:T(8,128)(2,1)}, bf16[64,3072]{1,0:T(8,128)(2,1)S(1)}, u32[]{:S(2)}, u32[]{:S(2)}) collective-permute-start(bf16[64,3072]{1,0:T(8,128)(2,1)} %get-tuple-element.14), channel_id=1, source_target_pairs={{0,16},{2,18},{4,20},{6,22},{8,24},{10,26},{12,28},{14,30},{1,17},... | collective-permute-start | bytes 1179656 | tf_op jit(solution)/shard_map/ppermute | solution.py:179
  435.8 51.8 %collective-permute-start.21 = (bf16[64,3072]{1,0:T(8,128)(2,1)S(1)}, bf16[64,3072]{1,0:T(8,128)(2,1)S(1)}, u32[]{:S(2)}, u32[]{:S(2)}) collective-permute-start(bf16[64,3072]{1,0:T(8,128)(2,1)S(1)} %get-tuple-element.7), channel_id=1, source_target_pairs={{0,18},{2,20},{4,22},{6,24},{8,26},{10,28},{12,30},{14,16},{1,19},... | collective-permute-start | bytes 1179656 | tf_op jit(solution)/shard_map/ppermute | solution.py:179
  437.1 50.4 %collective-permute-start.20 = (bf16[64,3072]{1,0:T(8,128)(2,1)S(1)}, bf16[64,3072]{1,0:T(8,128)(2,1)S(1)}, u32[]{:S(2)}, u32[]{:S(2)}) collective-permute-start(bf16[64,3072]{1,0:T(8,128)(2,1)S(1)} %get-tuple-element.8), channel_id=1, source_target_pairs={{0,20},{2,22},{4,24},{6,26},{8,28},{10,30},{12,16},{14,18},{1,21},... | collective-permute-start | bytes 1179656 | tf_op jit(solution)/shard_map/ppermute | solution.py:179
  438.4 49.1 %collective-permute-start.19 = (bf16[64,3072]{1,0:T(8,128)(2,1)S(1)}, bf16[64,3072]{1,0:T(8,128)(2,1)S(1)}, u32[]{:S(2)}, u32[]{:S(2)}) collective-permute-start(bf16[64,3072]{1,0:T(8,128)(2,1)S(1)} %get-tuple-element.9), channel_id=1, source_target_pairs={{0,22},{2,24},{4,26},{6,28},{8,30},{10,16},{12,18},{14,20},{1,23},... | collective-permute-start | bytes 1179656 | tf_op jit(solution)/shard_map/ppermute | solution.py:179
  439.7 47.7 %collective-permute-start.18 = (bf16[64,3072]{1,0:T(8,128)(2,1)}, bf16[64,3072]{1,0:T(8,128)(2,1)S(1)}, u32[]{:S(2)}, u32[]{:S(2)}) collective-permute-start(bf16[64,3072]{1,0:T(8,128)(2,1)} %get-tuple-element.10), channel_id=1, source_target_pairs={{0,24},{2,26},{4,28},{6,30},{8,16},{10,18},{12,20},{14,22},{1,25},... | collective-permute-start | bytes 1179656 | tf_op jit(solution)/shard_map/ppermute | solution.py:179
  456.9 11.9 %collective-permute-start.15 = (bf16[64,3072]{1,0:T(8,128)(2,1)}, bf16[64,3072]{1,0:T(8,128)(2,1)S(1)}, u32[]{:S(2)}, u32[]{:S(2)}) collective-permute-start(bf16[64,3072]{1,0:T(8,128)(2,1)} %get-tuple-element.13), channel_id=1, source_target_pairs={{0,30},{2,16},{4,18},{6,20},{8,22},{10,24},{12,26},{14,28},{1,31},... | collective-permute-start | bytes 1179656 | tf_op jit(solution)/shard_map/ppermute | solution.py:179
  468.8 8.4 %collective-permute-start.16 = (bf16[64,3072]{1,0:T(8,128)(2,1)}, bf16[64,3072]{1,0:T(8,128)(2,1)S(1)}, u32[]{:S(2)}, u32[]{:S(2)}) collective-permute-start(bf16[64,3072]{1,0:T(8,128)(2,1)} %get-tuple-element.12), channel_id=1, source_target_pairs={{0,28},{2,30},{4,16},{6,18},{8,20},{10,22},{12,24},{14,26},{1,29},... | collective-permute-start | bytes 1179656 | tf_op jit(solution)/shard_map/ppermute | solution.py:179
  477.2 10.2 %collective-permute-start.17 = (bf16[64,3072]{1,0:T(8,128)(2,1)}, bf16[64,3072]{1,0:T(8,128)(2,1)S(1)}, u32[]{:S(2)}, u32[]{:S(2)}) collective-permute-start(bf16[64,3072]{1,0:T(8,128)(2,1)} %get-tuple-element.11), channel_id=1, source_target_pairs={{0,26},{2,28},{4,30},{6,16},{8,18},{10,20},{12,22},{14,24},{1,27},... | collective-permute-start | bytes 1179656 | tf_op jit(solution)/shard_map/ppermute | solution.py:179
  (12 other events, 565.7 us)
Sparse Core Ops, SparseCore 0:
  90.2 85.4 all-gather.1
  330.2 77.0 reduce-scatter.1
  435.9 19.9 all-reduce.1
